TPU v7x, 32 devices: a whole 2x2x4 slice. The times are simulated.
32 devices in a mesh: section: 8 (over z, x), dp: 4 (over y, core).
Axes of the slice: x: 2, y: 2, z: 4, core: 2. Of those that a mesh axis runs over, the one named last changes fastest.
Arguments:
- acts: bfloat16 [8, 512, 2048], P('section', 'dp'), may hold values from -12 to 12
- weights: bfloat16 [8, 2048, 2048], P('section', 'dp'), may hold values from -6 to 6
- cotangent: bfloat16 [8, 512, 2048], P('section', 'dp'), may hold values from -20 to 20, as said below
Outputs:
- shadow: bfloat16 [8, 512, 2048], P('section', 'dp')
- back_grad: bfloat16 [8, 512, 2048], P('section', 'dp')
- successor_weights: bfloat16 [8, 2048, 2048], P('section', 'dp')
Inputs may be any that keep to these rules, and one draw needn't show every extreme that they name: `cotangent`: entries of order one; the typical size differs from section to section.
All inputs are finite; a program needn't handle non-finite values.
Results may differ from a plain program's by a relative error of at most 0.0047.
Values may be sent and summed in bfloat16 or wider, within the bound.
A program may use at most 64 MiB of HBM per device.

v0:
```python
import math

import jax
import jax.numpy as jnp
from jax import lax
from jax.sharding import PartitionSpec as P

step_rate = 0.5


def shifted(shard, axis, by):
    peers = lax.axis_size(axis)
    pairs = [(i, i + by) for i in range(peers) if 0 <= i + by < peers]
    return lax.ppermute(shard, axis, pairs)


def gelu_slope(pre):
    return jax.jvp(jax.nn.gelu, (pre,), (jnp.ones_like(pre),))[1]


def layer(inputs, matrix, root):
    pre = jnp.dot(inputs, matrix, preferred_element_type=jnp.float32) / root
    return ((inputs.astype(jnp.float32) + jax.nn.gelu(pre)).astype(jnp.bfloat16), pre)


def per_device(acts, weights, cotangent):
    inputs = acts[0]
    upstream = cotangent[0]
    own_rows = weights[0]
    width = inputs.shape[1]
    share = own_rows.shape[0]
    root = jnp.float32(math.sqrt(width))
    full_matrix = lax.all_gather(own_rows, "dp", axis=0, tiled=True)
    out_act, pre = layer(inputs, full_matrix, root)
    arrived = shifted(out_act, "section", 1)
    spare = layer(arrived, full_matrix, root)[0]
    pregrad = (upstream.astype(jnp.float32) * gelu_slope(pre)).astype(jnp.bfloat16)
    spread = lax.dot_general(
        pregrad, full_matrix, (((1,), (1,)), ((), ())), preferred_element_type=jnp.float32
    )
    input_grad = (upstream.astype(jnp.float32) + spread / root).astype(jnp.bfloat16)
    shadow_next = shifted(spare, "section", -1)
    grad_next = shifted(input_grad, "section", -1)
    feature_blocks = lax.all_to_all(inputs, "dp", split_axis=1, concat_axis=0, tiled=True)
    wgrad = lax.dot_general(
        feature_blocks,
        lax.all_gather(pregrad, "dp", axis=0, tiled=True),
        (((0,), (0,)), ((), ())),
        preferred_element_type=jnp.float32,
    )
    wgrad = wgrad / root
    energy = lax.psum(jnp.sum(wgrad * wgrad), ("section", "dp"))
    entries = jnp.float32(lax.axis_size("section") * lax.axis_size("dp") * share * width)
    scale = step_rate / jnp.sqrt(energy / entries + 1e-05)
    updated = (own_rows.astype(jnp.float32) - scale * wgrad).astype(jnp.bfloat16)
    weights_next = shifted(updated, "section", -1)
    return (shadow_next[None], grad_next[None], weights_next[None])


def solution(mesh):
    return jax.shard_map(
        per_device,
        mesh=mesh,
        in_specs=(P("section", "dp", None), P("section", "dp", None), P("section", "dp", None)),
        out_specs=(P("section", "dp", None), P("section", "dp", None), P("section", "dp", None)),
        check_vma=False,
    )
```

profile of v0, /device:TPU:0, one launch (start us, length us, event | category | flops | bytes accessed | tf_op | source)
XLA Modules:
  0.0 253.6 jit_solution(14239683830725967413)
XLA Ops:
  7.2 0.0 all-gather.6.cloned.1.call-start
  7.2 0.7 all-gather.6.cloned.1.call-update
  7.9 0.0 copy-start.4
  7.9 0.0 copy-start
  7.9 0.0 all-gather.4.cloned.1.call-start
  8.0 62.6 %all-gather.6.cloned.1.call-done = bf16[1,2048,2048]{2,1,0:T(8,128)(2,1)} async-done(((bf16[1,512,2048]{2,1,0:T(8,128)(2,1)}), bf16[1,2048,2048]{2,1,0:T(8,128)(2,1)}) %all-gather.6.cloned.1.call-update) | async-done | bytes 8388624 | tf_op jit(solution)/shard_map/all_gather | solution.py:33
  70.6 6.8 %fusion.22 = (bf16[128,2048]{1,0:T(8,128)(2,1)}, bf16[128,2048]{1,0:T(8,128)(2,1)}) fusion(bf16[1,128,2048]{2,1,0:T(8,128)(2,1)} %param.5, bf16[1,128,2048]{2,1,0:T(8,128)(2,1)} %param.3, bf16[1,2048,2048]{2,1,0:T(8,128)(2,1)} %all-gather.6.cloned.1.call-done), kind=kOutput, calls=%fused_computation.18 | convolution fusion | flops 1080033280 | bytes 10485760 | tf_op jit(solution)/shard_map/dot_general | solution.py:22
  77.4 0.0 all-gather.4.cloned.1.call-update
  77.4 0.0 copy-done.4
  77.5 1.0 copy.11
  78.5 3.5 %all-to-all-start = ((bf16[128,4,512]{0,2,1:T(8,128)(2,1)}), bf16[128,4,512]{0,2,1:T(8,128)(2,1)S(1)}, u32[]{:S(2)}, u32[]{:S(2)}) async-start(bf16[128,4,512]{0,2,1:T(8,128)(2,1)} %bitcast.7), calls=%async_computation | async-start | bytes 1048576 | tf_op jit(solution)/shard_map/all_to_all | solution.py:44
  82.0 0.0 copy-done
  82.0 2.5 copy.10
  84.5 10.0 %all-to-all-done = bf16[128,4,512]{0,2,1:T(8,128)(2,1)S(1)} async-done(((bf16[128,4,512]{0,2,1:T(8,128)(2,1)}), bf16[128,4,512]{0,2,1:T(8,128)(2,1)S(1)}, u32[]{:S(2)}, u32[]{:S(2)}) %all-to-all-start) | async-done | bytes 524320 | tf_op jit(solution)/shard_map/all_to_all | solution.py:44
  94.5 0.2 copy.12
  94.7 8.8 %all-gather.4.cloned.1.call-done = bf16[512,2048]{1,0:T(8,128)(2,1)} async-done(((bf16[128,2048]{1,0:T(8,128)(2,1)}), bf16[512,2048]{1,0:T(8,128)(2,1)}) %all-gather.4.cloned.1.call-update) | async-done | bytes 2097168 | tf_op jit(solution)/shard_map/all_gather | solution.py:47
  103.6 0.0 copy-start.1
  103.6 5.7 %multiply_reduce_fusion = (f32[]{:T(128)}, f32[2048,512]{1,0:T(8,128)}) fusion(bf16[512,2048]{1,0:T(8,128)(2,1)} %all-gather.4.cloned.1.call-done, bf16[512,512]{1,0:T(8,128)(2,1)S(1)} %bitcast.54), kind=kOutput, calls=%fused_computation.8 | convolution fusion | flops 1076887552 | bytes 6815748 | tf_op jit(solution)/shard_map/dot_general | solution.py:45
  109.2 39.5 %psum.7 = f32[]{:T(128)} all-reduce(f32[]{:T(128)} %get-tuple-element.14), channel_id=1, replica_groups=mesh['section'=8,'dp'=4] {'section','dp'}, use_global_device_ids=true, to_apply=%region_1.0 | all-reduce | flops 1 | bytes 8 | tf_op jit(solution)/shard_map/psum | solution.py:52
  149.4 0.0 copy-done.1
  149.4 0.0 copy-start.5
  149.5 0.0 copy-start.2
  149.5 0.0 copy-start.3
  149.5 0.0 slice-start
  149.5 3.1 %fusion.6 = bf16[512,2048]{0,1:T(8,128)(2,1)S(1)} fusion(f32[2048,512]{1,0:T(8,128)} %get-tuple-element.15, bf16[1,512,2048]{1,2,0:T(8,128)(2,1)S(1)} %copy-done.1, f32[]{:T(128)S(6)} %mul.84), kind=kLoop, calls=%fused_computation.7 | loop fusion | flops 4194304 | bytes 8388612 | tf_op jit(solution)/shard_map/convert_element_type | solution.py:55
  152.6 1.3 collective-permute-start.3
  153.9 0.0 copy-done.5
  153.9 0.0 slice-start.1
  153.9 5.1 %collective-permute-start = (bf16[128,2048]{1,0:T(8,128)(2,1)S(1)}, bf16[128,2048]{1,0:T(8,128)(2,1)S(1)}, u32[]{:S(2)}, u32[]{:S(2)}) collective-permute-start(bf16[128,2048]{1,0:T(8,128)(2,1)S(1)} %copy-done.5), channel_id=1, source_target_pairs={{0,4},{4,8},{8,12},{12,16},{16,20},{20,24},{24,28},{1,5},{5,9},{9,... | collective-permute-start | bytes 1572872 | tf_op jit(solution)/shard_map/ppermute | solution.py:14
  159.0 0.0 copy-done.2
  159.0 0.0 copy-done.3
  159.1 6.3 %fusion.19 = bf16[128,2048]{1,0:T(8,128)(2,1)S(1)} fusion(bf16[128,2048]{1,0:T(8,128)(2,1)S(1)} %copy-done.2, bf16[1,2048,2048]{2,1,0:T(8,128)(2,1)} %all-gather.6.cloned.1.call-done, bf16[1,128,2048]{2,1,0:T(8,128)(2,1)S(1)} %copy-done.3), kind=kOutput, calls=%fused_computation.13 | convolution fusion | flops 1074790400 | bytes 9961472 | tf_op jit(solution)/shard_map/dot_general | solution.py:38
  165.4 1.3 collective-permute-start.2
  166.7 57.8 %collective-permute-done = bf16[128,2048]{1,0:T(8,128)(2,1)S(1)} collective-permute-done((bf16[128,2048]{1,0:T(8,128)(2,1)S(1)}, bf16[128,2048]{1,0:T(8,128)(2,1)S(1)}, u32[]{:S(2)}, u32[]{:S(2)}) %collective-permute-start) | collective-permute-done | bytes 524320 | tf_op jit(solution)/shard_map/ppermute | solution.py:14
  224.5 0.0 slice-done
  224.5 0.0 slice-done.1
  224.5 1.8 add_convert_fusion
  226.3 1.3 collective-permute-start.1
  227.6 0.0 collective-permute-done.2
  227.6 15.2 %collective-permute-done.1 = bf16[128,2048]{1,0:T(8,128)(2,1)S(1)} collective-permute-done((bf16[128,2048]{1,0:T(8,128)(2,1)S(1)}, bf16[128,2048]{1,0:T(8,128)(2,1)S(1)}, u32[]{:S(2)}, u32[]{:S(2)}) %collective-permute-start.1) | collective-permute-done | bytes 524320 | tf_op jit(solution)/shard_map/ppermute | solution.py:14
  242.8 0.0 collective-permute-done.3
  242.8 2.4 copy.13
  245.1 0.8 copy.16
  245.9 0.8 copy.17
  (1 shorter events, 0.0 us)
Async XLA Ops:
  7.2 63.4 %all-gather.6.cloned.1.call-start = ((), (), s32[]{:S(2)}) async-start(), calls=%async_computation.2 | async-start | bytes 10485760 | tf_op jit(solution)/shard_map/all_gather | solution.py:33
  7.9 69.6 %copy-start.4 = (bf16[1,128,2048]{2,1,0:T(8,128)(2,1)S(1)}, bf16[1,128,2048]{2,1,0:T(8,128)(2,1)}, u32[]{:S(2)}) copy-start(bf16[1,128,2048]{2,1,0:T(8,128)(2,1)} %param.3) | copy-start | bytes 1572868
  7.9 74.1 %copy-start = (bf16[1,512,2048]{2,1,0:T(8,128)(2,1)S(1)}, bf16[1,512,2048]{2,1,0:T(8,128)(2,1)}, u32[]{:S(2)}) copy-start(bf16[1,512,2048]{2,1,0:T(8,128)(2,1)} %param.4) | copy-start | bytes 6291460
  7.9 95.6 %all-gather.4.cloned.1.call-start = ((), (), s32[]{:S(2)}) async-start(), calls=%async_computation.1 | async-start | bytes 2621440 | tf_op jit(solution)/shard_map/all_gather | solution.py:47
  78.5 16.0 %all-to-all-start = ((bf16[128,4,512]{0,2,1:T(8,128)(2,1)}), bf16[128,4,512]{0,2,1:T(8,128)(2,1)S(1)}, u32[]{:S(2)}, u32[]{:S(2)}) async-start(bf16[128,4,512]{0,2,1:T(8,128)(2,1)} %bitcast.7), calls=%async_computation | async-start | bytes 1048576 | tf_op jit(solution)/shard_map/all_to_all | solution.py:44
  103.6 45.9 %copy-start.1 = (bf16[1,512,2048]{1,2,0:T(8,128)(2,1)S(1)}, bf16[1,512,2048]{1,2,0:T(8,128)(2,1)}, u32[]{:S(2)}) copy-start(bf16[1,512,2048]{1,2,0:T(8,128)(2,1)} %copy.10) | copy-start | bytes 6291460
  149.4 4.5 %copy-start.5 = (bf16[128,2048]{1,0:T(8,128)(2,1)S(1)}, bf16[128,2048]{1,0:T(8,128)(2,1)}, u32[]{:S(2)}) copy-start(bf16[128,2048]{1,0:T(8,128)(2,1)} %get-tuple-element.13) | copy-start | bytes 1572868
  149.5 9.6 %copy-start.2 = (bf16[128,2048]{1,0:T(8,128)(2,1)S(1)}, bf16[128,2048]{1,0:T(8,128)(2,1)}, u32[]{:S(2)}) copy-start(bf16[128,2048]{1,0:T(8,128)(2,1)} %get-tuple-element.12) | copy-start | bytes 1572868
  149.5 9.6 %copy-start.3 = (bf16[1,128,2048]{2,1,0:T(8,128)(2,1)S(1)}, bf16[1,128,2048]{2,1,0:T(8,128)(2,1)}, u32[]{:S(2)}) copy-start(bf16[1,128,2048]{2,1,0:T(8,128)(2,1)} %param.5) | copy-start | bytes 1572868
  149.5 75.0 %slice-start = ((s8[8388608]{0:T(1024)(128)(4,1)}), s8[4194304]{0:T(1024)(128)(4,1)S(1)}, s32[]{:S(2)}) async-start(s8[8388608]{0:T(1024)(128)(4,1)} %bitcast.48), calls=%async_computation.3 | async-start | bytes 8388608
  152.6 90.2 %collective-permute-start.3 = (bf16[512,2048]{0,1:T(8,128)(2,1)S(1)}, bf16[512,2048]{0,1:T(8,128)(2,1)S(1)}, u32[]{:S(2)}, u32[]{:S(2)}) collective-permute-start(bf16[512,2048]{0,1:T(8,128)(2,1)S(1)} %fusion.6), channel_id=1, source_target_pairs={{4,0},{8,4},{12,8},{16,12},{20,16},{24,20},{28,24},{5,1},{9,5},{13... | collective-permute-start | bytes 6291464 | tf_op jit(solution)/shard_map/ppermute | solution.py:14
  153.9 70.6 %slice-start.1 = ((s8[8388608]{0:T(1024)(128)(4,1)}), s8[4194304]{0:T(1024)(128)(4,1)S(1)}, s32[]{:S(2)}) async-start(s8[8388608]{0:T(1024)(128)(4,1)} %bitcast.48), calls=%async_computation.4 | async-start | bytes 8388608
  153.9 70.6 %collective-permute-start = (bf16[128,2048]{1,0:T(8,128)(2,1)S(1)}, bf16[128,2048]{1,0:T(8,128)(2,1)S(1)}, u32[]{:S(2)}, u32[]{:S(2)}) collective-permute-start(bf16[128,2048]{1,0:T(8,128)(2,1)S(1)} %copy-done.5), channel_id=1, source_target_pairs={{0,4},{4,8},{8,12},{12,16},{16,20},{20,24},{24,28},{1,5},{5,9},{9,... | collective-permute-start | bytes 1572872 | tf_op jit(solution)/shard_map/ppermute | solution.py:14
  165.4 62.2 %collective-permute-start.2 = (bf16[128,2048]{1,0:T(8,128)(2,1)S(1)}, bf16[128,2048]{1,0:T(8,128)(2,1)S(1)}, u32[]{:S(2)}, u32[]{:S(2)}) collective-permute-start(bf16[128,2048]{1,0:T(8,128)(2,1)S(1)} %fusion.19), channel_id=1, source_target_pairs={{4,0},{8,4},{12,8},{16,12},{20,16},{24,20},{28,24},{5,1},{9,5},{13... | collective-permute-start | bytes 1572872 | tf_op jit(solution)/shard_map/ppermute | solution.py:14
  226.3 16.5 %collective-permute-start.1 = (bf16[128,2048]{1,0:T(8,128)(2,1)S(1)}, bf16[128,2048]{1,0:T(8,128)(2,1)S(1)}, u32[]{:S(2)}, u32[]{:S(2)}) collective-permute-start(bf16[128,2048]{1,0:T(8,128)(2,1)S(1)} %add_convert_fusion), channel_id=1, source_target_pairs={{4,0},{8,4},{12,8},{16,12},{20,16},{24,20},{28,24},{5,1},{9,5},{13... | collective-permute-start | bytes 1572872 | tf_op jit(solution)/shard_map/ppermute | solution.py:14
Sparse Core Ops, SparseCore 0:
  9.6 60.9 all-gather.5
  77.6 25.9 all-gather.3
where the time goes:
time: 254 us
  waiting for transfers between devices  155 us (61%)
  blocking collectives  39.5 us (16%)
  matrix products  20.6 us (8%)
  between operations  14.9 us (6%)
  starting transfers between devices  12.5 us (5%)
  local copies, waits for them, and re-layouts  7.75 us (3%)
  other arithmetic  3.1 us (1%)
    ppermute x4, waiting for transfers between devices, shifted(): return lax.ppermute(shard, axis, pairs)  73 us
    all_gather x1, waiting for transfers between devices, per_device(): full_matrix = lax.all_gather(own_rows, 'dp', axis=0, tiled=True)  62.6 us
    psum x1, blocking collectives, per_device(): energy = lax.psum(jnp.sum(wgrad * wgrad), ('section', 'dp'))  39.5 us
    all_to_all x1, waiting for transfers between devices, per_device(): lax.all_to_all(inputs, 'dp', split_axis=1, concat_axis=0, tiled=True)  9.99 us
    ppermute x4, starting transfers between devices, shifted(): return lax.ppermute(shard, axis, pairs)  8.98 us
    all_gather x1, waiting for transfers between devices, per_device(): lax.all_gather(pregrad, 'dp', axis=0, tiled=True)  8.84 us
    dot_general x2, matrix products, layer(): pre = jnp.dot(inputs, matrix, preferred_element_type=jnp.float32) / root  8.6 us
    unnamed x21, local copies, waits for them, and re-layouts  7.54 us
  transfers between devices with their start and end apart: 7, of which 5 were waited for; matrix products, arithmetic and copies ran while one was open for 5% of the time, Pallas kernels for 0%

commit v1 on v0

v1 whole, which is shorter than its diff:
```python
import functools
import math

import jax
import jax.numpy as jnp
from jax import lax
from jax.experimental import pallas as pl
from jax.experimental.pallas import tpu as pltpu
from jax.sharding import PartitionSpec as P

MESH = pl.DeviceIdType.MESH
step_rate = 0.5
GELU_A = math.sqrt(2.0 / math.pi)
GELU_B = 0.044715
F32 = jnp.float32
BF16 = jnp.bfloat16


def kernel(
    cfg, acts, w, cot, shadow, back, succ,
    wp, wn, xg, xn, ah, ch, cn, p1s, p1r, p2s, p2r, acc, oh, og, pgo, pgn, xt, wg,
    sps, spr, shs, e1, e2, es, ssem, rsem, lsem,
):
    S, n, t, D = cfg
    r, pairs, h = D // n, n // 2, D // 2
    R, tt, T = 2 * r, 2 * t, n * t
    half_pairs = max(pairs // 2, 1)
    inv_root = F32(1.0 / math.sqrt(D))
    s = lax.axis_index("section")
    j = lax.axis_index("dp")
    q, c = j // 2, j % 2
    other = 1 - c
    partner = (s, 2 * q + other)
    has_next = s < S - 1
    has_prev = s > 0
    first = s == 0
    prev = (lax.max(s - 1, 0), j)

    def rows(start, size):
        return pl.ds(pl.multiple_of(start, math.gcd(size, 128)), size)

    def cols(start, size):
        return pl.ds(pl.multiple_of(start, 128), size)

    def mate(d):
        return lax.rem(q + d, pairs)

    def source(d):
        return lax.rem(q - d + pairs, pairs)

    counts = {"s": 0, "r": 0}
    pending = []

    def fresh(kind, many=1):
        first_index = counts[kind]
        counts[kind] += many
        return first_index

    def when(pred, f):
        if pred is None:
            f()
        else:
            pl.when(pred)(f)

    def send(src, dst, recv_index, device, pred=None):
        index = fresh("s")

        def make():
            return pltpu.make_async_remote_copy(
                src_ref=src(), dst_ref=dst(), send_sem=ssem.at[index],
                recv_sem=rsem.at[recv_index], device_id=device, device_id_type=MESH,
            )

        when(pred, lambda: make().start())
        pending.append((pred, lambda: make().wait_send()))

    def recv(dst, recv_index):
        pltpu.make_async_remote_copy(
            src_ref=dst, dst_ref=dst, send_sem=ssem.at[0],
            recv_sem=rsem.at[recv_index], device_id=partner, device_id_type=MESH,
        ).wait_recv()

    barrier = pltpu.get_barrier_semaphore()
    for d in range(1, n):
        pl.semaphore_signal(barrier, inc=1, device_id=(s, lax.rem(j + d, n)), device_id_type=MESH)
    for d in range(1, S):
        pl.semaphore_signal(barrier, inc=1, device_id=(lax.rem(s + d, S), j), device_id_type=MESH)
    pl.semaphore_wait(barrier, (n - 1) + (S - 1))

    xd, xf = fresh("r", pairs), fresh("r", pairs)
    for d in range(1, pairs):
        send(lambda d=d: acts.at[:, cols(mate(d) * R, R)], lambda: xg.at[rows(j * t, t), :],
             xd + d, (s, 2 * mate(d) + c))
    send(lambda: acts.at[:, cols(q * R, R)], lambda: xg.at[rows(j * t, t), :], xf, partner)
    wpr = fresh("r")
    send(lambda: w, lambda: wp.at[rows(c * r, r), :], wpr, partner)
    ahr, chr_ = fresh("r"), fresh("r")
    send(lambda: acts.at[:, cols(other * h, h)], lambda: ah.at[rows(c * t, t), :], ahr, partner)
    send(lambda: cot.at[:, cols(other * h, h)], lambda: ch.at[rows(c * t, t), :], chr_, partner)
    wnr, wnf, xnr, pgr, cnr = (fresh("r") for _ in range(5))
    send(lambda: w, lambda: wn.at[rows(c * r, r), :], wnr, prev, has_prev)

    local = [
        pltpu.make_async_copy(w, wp.at[rows(c * r, r), :], lsem.at[0]),
        pltpu.make_async_copy(acts.at[:, cols(q * R, R)], xg.at[rows(j * t, t), :], lsem.at[1]),
        pltpu.make_async_copy(acts.at[:, cols(c * h, h)], ah.at[rows(c * t, t), :], lsem.at[2]),
        pltpu.make_async_copy(cot.at[:, cols(c * h, h)], ch.at[rows(c * t, t), :], lsem.at[3]),
    ]
    for copy in local:
        copy.start()
    for copy in local:
        copy.wait()

    def xrows(d, core):
        return xg.at[rows((2 * source(d) + core) * t, t), :]

    for d in range(1, pairs):
        recv(xrows(d, c), xd + d)
        send(lambda d=d: xrows(d, c), lambda d=d: xrows(d, c), xf + d, partner)
    for d in range(pairs):
        recv(xrows(d, other), xf + d)
    recv(wp.at[rows(other * r, r), :], wpr)
    send(lambda: xg.at[:, cols(c * r, r)], lambda: xn, xnr, prev, has_prev)

    step = min(256, h)

    def partials(gathered, matrix, out, landing, base, pred):
        for d in list(range(1, pairs)) + [0]:
            def body(k, carry, d=d):
                value = jnp.dot(
                    gathered[rows(mate(d) * tt, tt), :], matrix[:, cols(c * h + k * step, step)],
                    preferred_element_type=F32,
                )
                if d:
                    out[d, :, cols(k * step, step)] = value.astype(BF16)
                else:
                    acc[:, cols(k * step, step)] = value
                return carry

            when(pred, lambda body=body: lax.fori_loop(0, h // step, body, None))
            if d:
                send(lambda d=d: out.at[d], lambda d=d: landing.at[d], base + d,
                     (s, 2 * mate(d) + c), pred)

    f1 = fresh("r", pairs)
    partials(xg, wp, p1s, p1r, f1, None)
    recv(ah.at[rows(other * t, t), :], ahr)
    recv(ch.at[rows(other * t, t), :], chr_)
    for d in range(1, pairs):
        recv(p1r.at[d], f1 + d)

    def total(landing, here):
        pre = acc[here, :]
        for d in range(1, pairs):
            pre += landing[d, here, :].astype(F32)
        return pre * inv_root

    def tanh_of(pre):
        return jnp.tanh(F32(GELU_A) * (pre + F32(GELU_B) * (pre * pre * pre)))

    def act_body(i, carry):
        here = rows(i * 16, 16)
        pre = total(p1r, here)
        th = tanh_of(pre)
        oh[here, :] = (ah[here, :].astype(F32) + 0.5 * pre * (1.0 + th)).astype(BF16)
        slope = 0.5 * (1.0 + th) + 0.5 * pre * (1.0 - th * th) * (
            F32(GELU_A) * (1.0 + F32(3.0 * GELU_B) * (pre * pre)))
        pgo[c, rows(q * tt + i * 16, 16), :] = (ch[here, :].astype(F32) * slope).astype(BF16)
        return carry

    lax.fori_loop(0, tt // 16, act_body, None)

    def block(buf, half, qq):
        return buf.at[half, rows(qq * tt, tt), :]

    send(lambda: block(pgo, c, q), lambda: block(pgn, c, q), pgr, prev, has_prev)
    od, of, nd, nf = (fresh("r", pairs) for _ in range(4))

    def gather_start(buf, direct, forward, pred):
        for d in range(1, pairs):
            send(lambda: block(buf, c, q), lambda: block(buf, c, q), direct + d,
                 (s, 2 * mate(d) + c), pred)
        send(lambda: block(buf, c, q), lambda: block(buf, c, q), forward, partner, pred)

    def gather_end(buf, direct, forward, pred):
        for d in range(1, pairs):
            when(pred, lambda d=d: recv(block(buf, c, source(d)), direct + d))
            send(lambda d=d: block(buf, c, source(d)), lambda d=d: block(buf, c, source(d)),
                 forward + d, partner, pred)
        for d in range(pairs):
            when(pred, lambda d=d: recv(block(buf, other, source(d)), forward + d))

    gather_start(pgo, od, of, first)

    ogd, ogf = fresh("r", pairs), fresh("r", pairs)
    ours = q // half_pairs == c
    leads = jnp.logical_and(has_next, ours)
    follows = jnp.logical_and(has_next, jnp.logical_not(ours))

    def orows(qq):
        return og.at[rows(qq * tt, tt), :]

    for m in range(half_pairs):
        qq = c * half_pairs + m
        send(lambda m=m: oh.at[:, cols(m * R, R)], lambda: orows(q), ogd + q, (s, 2 * qq + c),
             jnp.logical_and(has_next, qq != q))
    send(lambda: cot, lambda: cn, cnr, prev, has_prev)

    @pl.when(leads)
    def _():
        copy = pltpu.make_async_copy(
            oh.at[:, cols(lax.rem(q, half_pairs) * R, R)], orows(q), lsem.at[0])
        copy.start()
        copy.wait()

    send(lambda: orows(q), lambda: orows(q), ogf, partner, leads)
    for d in range(1, pairs):
        when(leads, lambda d=d: recv(orows(source(d)), ogd + source(d)))
        send(lambda d=d: orows(source(d)), lambda d=d: orows(source(d)), ogf + d, partner, leads)
    for d in range(pairs):
        when(follows, lambda d=d: recv(orows(source(d)), ogf + d))

    wstep = min(256, h)

    def wgrad(buf, store):
        def body(k, total_sq):
            total_sq = total_sq
            for half in range(2):
                value = jnp.dot(xt[...], buf[half, :, cols(k * wstep, wstep)],
                                preferred_element_type=F32) * inv_root
                if store:
                    wg[:, cols(half * h + k * wstep, wstep)] = value
                total_sq = total_sq + jnp.sum(
                    (value * value).reshape(r // 8, 8, wstep), axis=0)
            return total_sq

        total_sq = lax.fori_loop(0, h // wstep, body, jnp.zeros((8, wstep), F32))
        tile = total_sq[:, :128]
        for k in range(1, wstep // 128):
            tile = tile + total_sq[:, k * 128:(k + 1) * 128]
        es[0] = es[0] + tile

    es[0] = jnp.zeros((8, 128), F32)
    gather_end(pgo, od, of, first)

    @pl.when(first)
    def _():
        xt[...] = jnp.transpose(xg[:, cols(c * r, r)])
        wgrad(pgo, False)

    @pl.when(has_next)
    def _():
        recv(block(pgn, c, q), pgr)

    gather_start(pgn, nd, nf, has_next)

    @pl.when(has_next)
    def _():
        recv(xn, xnr)
        xt[...] = jnp.transpose(xn[...])

    gather_end(pgn, nd, nf, has_next)

    @pl.when(has_next)
    def _():
        wgrad(pgn, True)

    e1r = fresh("r", n)
    for d in range(1, n):
        send(lambda: es.at[0], lambda d=d: e1.at[d], e1r + d, (s, lax.rem(j + d, n)))
    sum1 = es[0]
    for d in range(1, n):
        recv(e1.at[d], e1r + d)
        sum1 = sum1 + e1[d]
    es[1] = sum1
    e2r = fresh("r", S)
    for d in range(1, S):
        send(lambda: es.at[1], lambda d=d: e2.at[d], e2r + d, (lax.rem(s + d, S), j))

    own_rows = rows(c * r, r)

    @pl.when(has_next)
    def _():
        recv(wn.at[own_rows, :], wnr)

    send(lambda: wn.at[own_rows, :], lambda: wn.at[own_rows, :], wnf, partner, has_next)
    spr_base = fresh("r", n)

    def tile_of(dd):
        return sps.at[dd]

    for d in list(range(1, pairs)) + [0]:
        def spread(d=d):
            value = jnp.zeros((tt, r), F32)
            for half in range(2):
                value = value + lax.dot_general(
                    pgn[half, rows(mate(d) * tt, tt), :], wn[own_rows, half * h:(half + 1) * h],
                    (((1,), (1,)), ((), ())), preferred_element_type=F32)
            sps[2 * d] = (value[:t] * inv_root).astype(BF16)
            sps[2 * d + 1] = (value[t:] * inv_root).astype(BF16)

        when(has_next, spread)
        for core in range(2):
            target = 2 * mate(d) + core
            mine = target == j
            send(lambda d=d, core=core: sps.at[2 * d + core], lambda: spr.at[:, cols(j * r, r)],
                 spr_base + j, (s, target),
                 has_next if d else jnp.logical_and(has_next, jnp.logical_not(mine)))

    @pl.when(has_next)
    def _():
        copy = pltpu.make_async_copy(sps.at[c], spr.at[:, cols(j * r, r)], lsem.at[0])
        copy.start()
        copy.wait()
        recv(wn.at[rows(other * r, r), :], wnf)

    f2 = fresh("r", pairs)
    partials(og, wn, p2s, p2r, f2, has_next)

    sum2 = es[1]
    for d in range(1, S):
        recv(e2.at[d], e2r + d)
        sum2 = sum2 + e2[d]
    energy = jnp.sum(jnp.sum(sum2, axis=0, keepdims=True), axis=1, keepdims=True)
    scale = step_rate / jnp.sqrt(energy / F32(S * D * D) + F32(1e-05))

    @pl.when(has_next)
    def _():
        def update(i, carry):
            here = rows(i * 16, 16)
            old = wn[rows(c * r + i * 16, 16), :].astype(F32)
            succ[here, :] = (old - scale * wg[here, :]).astype(BF16)
            return carry

        lax.fori_loop(0, r // 16, update, None)
        for d in range(1, n):
            owner = lax.rem(j + d, n)
            recv(spr.at[:, cols(owner * r, r)], spr_base + owner)
        recv(cn, cnr)

        def add(i, carry):
            here = rows(i * 16, 16)
            back[here, :] = (cn[here, :].astype(F32) + spr[here, :].astype(F32)).astype(BF16)
            return carry

        lax.fori_loop(0, t // 16, add, None)
        for d in range(1, pairs):
            recv(p2r.at[d], f2 + d)

        def shade(i, carry):
            here = rows(i * 16, 16)
            pre = total(p2r, here)
            shs[here, :] = (oh[here, :].astype(F32)
                            + 0.5 * pre * (1.0 + tanh_of(pre))).astype(BF16)
            return carry

        lax.fori_loop(0, tt // 16, shade, None)

    shr = fresh("r")
    send(lambda: shs.at[rows(other * t, t), :], lambda: shadow.at[:, cols(c * h, h)], shr,
         partner, has_next)

    @pl.when(has_next)
    def _():
        copy = pltpu.make_async_copy(
            shs.at[rows(c * t, t), :], shadow.at[:, cols(c * h, h)], lsem.at[0])
        copy.start()
        copy.wait()
        recv(shadow.at[:, cols(other * h, h)], shr)

    @pl.when(jnp.logical_not(has_next))
    def _():
        def clear(i, carry):
            succ[rows(i * 16, 16), :] = jnp.zeros((16, D), BF16)
            return carry

        def clear_tokens(i, carry):
            shadow[rows(i * 16, 16), :] = jnp.zeros((16, D), BF16)
            back[rows(i * 16, 16), :] = jnp.zeros((16, D), BF16)
            return carry

        lax.fori_loop(0, r // 16, clear, None)
        lax.fori_loop(0, t // 16, clear_tokens, None)

    for pred, wait in pending:
        when(pred, wait)


def per_device(S, n, acts, weights, cotangent):
    t, D = acts.shape[1:]
    r, pairs, h = D // n, n // 2, D // 2
    R, tt, T = 2 * r, 2 * t, n * t
    sems = 10 * pairs + 4 * n + 2 * S + 24
    vmem = pl.BlockSpec(memory_space=pltpu.VMEM)
    shadow, back, succ = pl.pallas_call(
        functools.partial(kernel, (S, n, t, D)),
        out_shape=(
            jax.ShapeDtypeStruct((t, D), BF16),
            jax.ShapeDtypeStruct((t, D), BF16),
            jax.ShapeDtypeStruct((r, D), BF16),
        ),
        in_specs=[vmem] * 3,
        out_specs=(vmem,) * 3,
        scratch_shapes=[
            pltpu.VMEM((R, D), BF16),
            pltpu.VMEM((R, D), BF16),
            pltpu.VMEM((T, R), BF16),
            pltpu.VMEM((T, r), BF16),
            pltpu.VMEM((tt, h), BF16),
            pltpu.VMEM((tt, h), BF16),
            pltpu.VMEM((t, D), BF16),
            pltpu.VMEM((pairs, tt, h), BF16),
            pltpu.VMEM((pairs, tt, h), BF16),
            pltpu.VMEM((pairs, tt, h), BF16),
            pltpu.VMEM((pairs, tt, h), BF16),
            pltpu.VMEM((tt, h), F32),
            pltpu.VMEM((tt, h), BF16),
            pltpu.VMEM((T, R), BF16),
            pltpu.VMEM((2, T, h), BF16),
            pltpu.VMEM((2, T, h), BF16),
            pltpu.VMEM((r, T), BF16),
            pltpu.VMEM((r, D), F32),
            pltpu.VMEM((n, t, r), BF16),
            pltpu.VMEM((t, D), BF16),
            pltpu.VMEM((tt, h), BF16),
            pltpu.VMEM((n, 8, 128), F32),
            pltpu.VMEM((S, 8, 128), F32),
            pltpu.VMEM((2, 8, 128), F32),
            pltpu.SemaphoreType.DMA((sems,)),
            pltpu.SemaphoreType.DMA((sems,)),
            pltpu.SemaphoreType.DMA((4,)),
        ],
        compiler_params=pltpu.CompilerParams(
            collective_id=0, has_side_effects=True, vmem_limit_bytes=60 * 1024 * 1024
        ),
        name="relay",
    )(acts[0], weights[0], cotangent[0])
    return shadow[None], back[None], succ[None]


def solution(mesh):
    spec = P("section", "dp", None)
    return jax.shard_map(
        functools.partial(per_device, mesh.shape["section"], mesh.shape["dp"]),
        mesh=mesh,
        in_specs=(spec, spec, spec),
        out_specs=(spec, spec, spec),
        check_vma=False,
    )
```

time: 254 us -> 125 us (0.49)
  waiting for transfers between devices: 155 us -> 0 us
  Pallas kernels: 0 us -> 119 us
  blocking collectives: 39.5 us -> 0 us
  matrix products: 20.6 us -> 0 us
  between operations: 14.9 us -> 0.65 us
  starting transfers between devices: 12.5 us -> 0 us
  other arithmetic: 3.1 us -> 0 us
    pallas_call x0 -> x1, Pallas kernels: none -> 119 us  [per_device(): pl.pallas_call(functools.partial(kernel, (S, n, t, D)), out_shape=(jax.Sh...]
    ppermute x4 -> x0, waiting for transfers between devices: 73 us -> none  [shifted(): return lax.ppermute(shard, axis, pairs)]
    all_gather x2 -> x0, waiting for transfers between devices: 71.5 us -> none  [the longest x1 62.6 us: per_device(): full_matrix = lax.all_gather(own_rows, 'dp', axis=0, tiled=True)]
    psum x1 -> x0, blocking collectives: 39.5 us -> none  [per_device(): energy = lax.psum(jnp.sum(wgrad * wgrad), ('section', 'dp'))]
    dot_general x4 -> x0, matrix products: 20.6 us -> none  [the longest x2 8.6 us: layer(): pre = jnp.dot(inputs, matrix, preferred_element_type=jnp.float32) / root]
    all_to_all x1 -> x0, waiting for transfers between devices: 9.99 us -> none  [per_device(): lax.all_to_all(inputs, 'dp', split_axis=1, concat_axis=0, tiled=True)]
    ppermute x4 -> x0, starting transfers between devices: 8.98 us -> none  [shifted(): return lax.ppermute(shard, axis, pairs)]
    all_to_all x1 -> x0, starting transfers between devices: 3.47 us -> none  [per_device(): lax.all_to_all(inputs, 'dp', split_axis=1, concat_axis=0, tiled=True)]
  transfers between devices with their start and end apart: 7 -> 0, of which waited for: 5 -> 0; matrix products, arithmetic and copies ran while one was open for 5% -> 0% of each run, Pallas kernels for 0% -> 0%
where the time goes in v1:
time: 125 us
  Pallas kernels  119 us (95%)
  local copies, waits for them, and re-layouts  5.23 us (4%)
    pallas_call x1, Pallas kernels, per_device(): pl.pallas_call(functools.partial(kernel, (S, n, t, D)), out_shape=(jax.Sh...  119 us
    unnamed x5, local copies, waits for them, and re-layouts  5.23 us

profile of v1, /device:TPU:0, one launch (start us, length us, event | category | flops | bytes accessed | tf_op | source)
XLA Modules:
  0.0 125.0 jit_solution(18078314679625373955)
XLA Ops:
  0.6 119.1 %relay.1 = (bf16[128,2048]{1,0:T(8,128)(2,1)}, bf16[128,2048]{1,0:T(8,128)(2,1)}, bf16[512,2048]{1,0:T(8,128)(2,1)}) custom-call(bf16[128,2048]{1,0:T(8,128)(2,1)} %bitcast.10, bf16[512,2048]{1,0:T(8,128)(2,1)} %bitcast.6, bf16[128,2048]{1,0:T(8,128)(2,1)} %bitcast.11), custom_call_target="tpu_custom_call" | custom-call | tf_op jit(solution)/shard_map/relay/pallas_call | solution.py:395
  119.8 0.0 copy-start
  119.8 2.0 %copy.9 = bf16[1,128,2048]{2,1,0:T(8,128)(2,1)} copy(bf16[1,128,2048]{2,1,0:T(8,128)(2,1)} %bitcast.9) | data formatting | bytes 1048576
  121.8 1.9 %copy.10 = bf16[1,128,2048]{2,1,0:T(8,128)(2,1)} copy(bf16[1,128,2048]{2,1,0:T(8,128)(2,1)} %bitcast.8) | data formatting | bytes 1048576
  123.7 0.0 copy-done
  123.7 1.3 %copy.11 = bf16[1,512,2048]{2,1,0:T(8,128)(2,1)} copy(bf16[1,512,2048]{2,1,0:T(8,128)(2,1)S(1)} %bitcast.7) | data formatting | bytes 4194304
Async XLA Ops:
  119.8 3.9 %copy-start = (bf16[512,2048]{1,0:T(8,128)(2,1)S(1)}, bf16[512,2048]{1,0:T(8,128)(2,1)}, u32[]{:S(2)}) copy-start(bf16[512,2048]{1,0:T(8,128)(2,1)} %get-tuple-element.8) | copy-start | bytes 6291460

commit v2 on v1

--- a/solution.py
+++ b/solution.py
@@ -19,12 +19,14 @@
 def kernel(
     cfg, acts, w, cot, shadow, back, succ,
     wp, wn, xg, xn, ah, ch, cn, p1s, p1r, p2s, p2r, acc, oh, og, pgo, pgn, xt, wg,
-    sps, spr, shs, e1, e2, es, ssem, rsem, lsem,
+    sps, spr, shs, su, bk, e1, e2, es, ssem, rsem, lsem,
 ):
     S, n, t, D = cfg
     r, pairs, h = D // n, n // 2, D // 2
     R, tt, T = 2 * r, 2 * t, n * t
     half_pairs = max(pairs // 2, 1)
+    pieces = 4
+    piece = h // pieces
     inv_root = F32(1.0 / math.sqrt(D))
     s = lax.axis_index("section")
     j = lax.axis_index("dp")
@@ -80,6 +82,15 @@
             recv_sem=rsem.at[recv_index], device_id=partner, device_id_type=MESH,
         ).wait_recv()
 
+    local = [
+        pltpu.make_async_copy(w.at[:, cols(c * h, h)], wp.at[rows(c * r, r), :], lsem.at[0]),
+        pltpu.make_async_copy(acts.at[:, cols(q * R, R)], xg.at[rows(j * t, t), :], lsem.at[1]),
+        pltpu.make_async_copy(acts.at[:, cols(c * h, h)], ah.at[rows(c * t, t), :], lsem.at[2]),
+        pltpu.make_async_copy(cot.at[:, cols(c * h, h)], ch.at[rows(c * t, t), :], lsem.at[3]),
+    ]
+    for copy in local:
+        copy.start()
+
     barrier = pltpu.get_barrier_semaphore()
     for d in range(1, n):
         pl.semaphore_signal(barrier, inc=1, device_id=(s, lax.rem(j + d, n)), device_id_type=MESH)
@@ -93,23 +104,23 @@
              xd + d, (s, 2 * mate(d) + c))
     send(lambda: acts.at[:, cols(q * R, R)], lambda: xg.at[rows(j * t, t), :], xf, partner)
     wpr = fresh("r")
-    send(lambda: w, lambda: wp.at[rows(c * r, r), :], wpr, partner)
+    send(lambda: w.at[:, cols(other * h, h)], lambda: wp.at[rows(c * r, r), :], wpr, partner)
     ahr, chr_ = fresh("r"), fresh("r")
     send(lambda: acts.at[:, cols(other * h, h)], lambda: ah.at[rows(c * t, t), :], ahr, partner)
     send(lambda: cot.at[:, cols(other * h, h)], lambda: ch.at[rows(c * t, t), :], chr_, partner)
-    wnr, wnf, xnr, pgr, cnr = (fresh("r") for _ in range(5))
-    send(lambda: w, lambda: wn.at[rows(c * r, r), :], wnr, prev, has_prev)
-
-    local = [
-        pltpu.make_async_copy(w, wp.at[rows(c * r, r), :], lsem.at[0]),
-        pltpu.make_async_copy(acts.at[:, cols(q * R, R)], xg.at[rows(j * t, t), :], lsem.at[1]),
-        pltpu.make_async_copy(acts.at[:, cols(c * h, h)], ah.at[rows(c * t, t), :], lsem.at[2]),
-        pltpu.make_async_copy(cot.at[:, cols(c * h, h)], ch.at[rows(c * t, t), :], lsem.at[3]),
-    ]
-    for copy in local:
-        copy.start()
-    for copy in local:
-        copy.wait()
+    xnr, pgr, cnr = (fresh("r") for _ in range(3))
+    wnr, wnf = fresh("r", 2 * pieces), fresh("r", pieces)
+    own_rows = rows(c * r, r)
+
+    def relay_weights(ks):
+        for k in ks:
+            for half in range(2):
+                here = pl.ds(half * h + k * piece, piece)
+                send(lambda here=here: w.at[:, here], lambda here=here: wn.at[own_rows, here],
+                     wnr + 2 * k + half, prev, has_prev)
+
+    early, late = range(pieces // 2), range(pieces // 2, pieces)
+    relay_weights(early)
 
     def xrows(d, core):
         return xg.at[rows((2 * source(d) + core) * t, t), :]
@@ -120,30 +131,32 @@
     for d in range(pairs):
         recv(xrows(d, other), xf + d)
     recv(wp.at[rows(other * r, r), :], wpr)
+
+    for copy in local:
+        copy.wait()
     send(lambda: xg.at[:, cols(c * r, r)], lambda: xn, xnr, prev, has_prev)
 
     step = min(256, h)
 
-    def partials(gathered, matrix, out, landing, base, pred):
-        for d in list(range(1, pairs)) + [0]:
-            def body(k, carry, d=d):
-                value = jnp.dot(
-                    gathered[rows(mate(d) * tt, tt), :], matrix[:, cols(c * h + k * step, step)],
-                    preferred_element_type=F32,
-                )
-                if d:
-                    out[d, :, cols(k * step, step)] = value.astype(BF16)
-                else:
-                    acc[:, cols(k * step, step)] = value
-                return carry
-
-            when(pred, lambda body=body: lax.fori_loop(0, h // step, body, None))
-            if d:
-                send(lambda d=d: out.at[d], lambda d=d: landing.at[d], base + d,
-                     (s, 2 * mate(d) + c), pred)
+    def product(gathered, matrix, at, out, d, k, width):
+        value = jnp.dot(
+            gathered[rows(mate(d) * tt, tt), :], matrix[:, cols(at + k * width, width)],
+            preferred_element_type=F32,
+        )
+        if d:
+            out[d, :, cols(k * width, width)] = value.astype(BF16)
+        else:
+            acc[:, cols(k * width, width)] = value
 
     f1 = fresh("r", pairs)
-    partials(xg, wp, p1s, p1r, f1, None)
+    for d in list(range(1, pairs)) + [0]:
+        def body(k, carry, d=d):
+            product(xg, wp, 0, p1s, d, k, step)
+            return carry
+
+        lax.fori_loop(0, h // step, body, None)
+        if d:
+            send(lambda d=d: p1s.at[d], lambda d=d: p1r.at[d], f1 + d, (s, 2 * mate(d) + c))
     recv(ah.at[rows(other * t, t), :], ahr)
     recv(ch.at[rows(other * t, t), :], chr_)
     for d in range(1, pairs):
@@ -174,6 +187,7 @@
         return buf.at[half, rows(qq * tt, tt), :]
 
     send(lambda: block(pgo, c, q), lambda: block(pgn, c, q), pgr, prev, has_prev)
+    relayed = pending.pop()
     od, of, nd, nf = (fresh("r", pairs) for _ in range(4))
 
     def gather_start(buf, direct, forward, pred):
@@ -204,7 +218,6 @@
         qq = c * half_pairs + m
         send(lambda m=m: oh.at[:, cols(m * R, R)], lambda: orows(q), ogd + q, (s, 2 * qq + c),
              jnp.logical_and(has_next, qq != q))
-    send(lambda: cot, lambda: cn, cnr, prev, has_prev)
 
     @pl.when(leads)
     def _():
@@ -219,6 +232,30 @@
         send(lambda d=d: orows(source(d)), lambda d=d: orows(source(d)), ogf + d, partner, leads)
     for d in range(pairs):
         when(follows, lambda d=d: recv(orows(source(d)), ogf + d))
+
+    f2 = fresh("r", pairs * pieces)
+
+    def shadow_pieces(ks):
+        for k in ks:
+            @pl.when(has_next)
+            def _(k=k):
+                for half in range(2):
+                    recv(wn.at[own_rows, half * h + k * piece:half * h + (k + 1) * piece],
+                         wnr + 2 * k + half)
+
+            theirs = cols(other * h + k * piece, piece)
+            send(lambda theirs=theirs: wn.at[own_rows, theirs],
+                 lambda theirs=theirs: wn.at[own_rows, theirs], wnf + k, partner, has_next)
+        for k in ks:
+            here = pl.ds(k * piece, piece)
+            when(has_next, lambda k=k: recv(
+                wn.at[rows(other * r, r), cols(c * h + k * piece, piece)], wnf + k))
+            for d in list(range(1, pairs)) + [0]:
+                when(has_next, lambda k=k, d=d: product(og, wn, c * h, p2s, d, k, piece))
+                if d:
+                    send(lambda d=d, here=here: p2s.at[d, :, here],
+                         lambda d=d, here=here: p2r.at[d, :, here],
+                         f2 + d * pieces + k, (s, 2 * mate(d) + c), has_next)
 
     wstep = min(256, h)
 
@@ -241,18 +278,22 @@
         es[0] = es[0] + tile
 
     es[0] = jnp.zeros((8, 128), F32)
+    shadow_pieces(early)
+
+    @pl.when(has_next)
+    def _():
+        recv(block(pgn, c, q), pgr)
+
+    gather_start(pgn, nd, nf, has_next)
+    when(*relayed)
+    relay_weights(late)
+    send(lambda: cot, lambda: cn, cnr, prev, has_prev)
     gather_end(pgo, od, of, first)
 
     @pl.when(first)
     def _():
         xt[...] = jnp.transpose(xg[:, cols(c * r, r)])
         wgrad(pgo, False)
-
-    @pl.when(has_next)
-    def _():
-        recv(block(pgn, c, q), pgr)
-
-    gather_start(pgn, nd, nf, has_next)
 
     @pl.when(has_next)
     def _():
@@ -277,13 +318,7 @@
     for d in range(1, S):
         send(lambda: es.at[1], lambda d=d: e2.at[d], e2r + d, (lax.rem(s + d, S), j))
 
-    own_rows = rows(c * r, r)
-
-    @pl.when(has_next)
-    def _():
-        recv(wn.at[own_rows, :], wnr)
-
-    send(lambda: wn.at[own_rows, :], lambda: wn.at[own_rows, :], wnf, partner, has_next)
+    shadow_pieces(late)
     spr_base = fresh("r", n)
 
     def tile_of(dd):
@@ -312,10 +347,6 @@
         copy = pltpu.make_async_copy(sps.at[c], spr.at[:, cols(j * r, r)], lsem.at[0])
         copy.start()
         copy.wait()
-        recv(wn.at[rows(other * r, r), :], wnf)
-
-    f2 = fresh("r", pairs)
-    partials(og, wn, p2s, p2r, f2, has_next)
 
     sum2 = es[1]
     for d in range(1, S):
@@ -329,10 +360,11 @@
         def update(i, carry):
             here = rows(i * 16, 16)
             old = wn[rows(c * r + i * 16, 16), :].astype(F32)
-            succ[here, :] = (old - scale * wg[here, :]).astype(BF16)
+            su[here, :] = (old - scale * wg[here, :]).astype(BF16)
             return carry
 
         lax.fori_loop(0, r // 16, update, None)
+        pltpu.make_async_copy(su, succ, lsem.at[1]).start()
         for d in range(1, n):
             owner = lax.rem(j + d, n)
             recv(spr.at[:, cols(owner * r, r)], spr_base + owner)
@@ -340,12 +372,14 @@
 
         def add(i, carry):
             here = rows(i * 16, 16)
-            back[here, :] = (cn[here, :].astype(F32) + spr[here, :].astype(F32)).astype(BF16)
+            bk[here, :] = (cn[here, :].astype(F32) + spr[here, :].astype(F32)).astype(BF16)
             return carry
 
         lax.fori_loop(0, t // 16, add, None)
+        pltpu.make_async_copy(bk, back, lsem.at[2]).start()
         for d in range(1, pairs):
-            recv(p2r.at[d], f2 + d)
+            for k in range(pieces):
+                recv(p2r.at[d, :, k * piece:(k + 1) * piece], f2 + d * pieces + k)
 
         def shade(i, carry):
             here = rows(i * 16, 16)
@@ -371,27 +405,39 @@
     @pl.when(jnp.logical_not(has_next))
     def _():
         def clear(i, carry):
-            succ[rows(i * 16, 16), :] = jnp.zeros((16, D), BF16)
+            su[rows(i * 16, 16), :] = jnp.zeros((16, D), BF16)
             return carry
 
         def clear_tokens(i, carry):
-            shadow[rows(i * 16, 16), :] = jnp.zeros((16, D), BF16)
-            back[rows(i * 16, 16), :] = jnp.zeros((16, D), BF16)
+            bk[rows(i * 16, 16), :] = jnp.zeros((16, D), BF16)
             return carry
 
         lax.fori_loop(0, r // 16, clear, None)
         lax.fori_loop(0, t // 16, clear_tokens, None)
-
+        pltpu.make_async_copy(su, succ, lsem.at[1]).start()
+        pltpu.make_async_copy(bk, back, lsem.at[2]).start()
+        copy = pltpu.make_async_copy(bk, shadow, lsem.at[0])
+        copy.start()
+        copy.wait()
+
+    pltpu.make_async_copy(su, succ, lsem.at[1]).wait()
+    pltpu.make_async_copy(bk, back, lsem.at[2]).wait()
     for pred, wait in pending:
         when(pred, wait)
+
+
+def hand_over(a, b, d, a_out, b_out, d_out):
+    a_out[...] = a[...]
+    b_out[...] = b[...]
+    d_out[...] = d[...]
 
 
 def per_device(S, n, acts, weights, cotangent):
     t, D = acts.shape[1:]
     r, pairs, h = D // n, n // 2, D // 2
     R, tt, T = 2 * r, 2 * t, n * t
-    sems = 10 * pairs + 4 * n + 2 * S + 24
-    vmem = pl.BlockSpec(memory_space=pltpu.VMEM)
+    sems = 15 * pairs + 4 * n + 2 * S + 40
+    held = pl.BlockSpec(memory_space=pl.ANY)
     shadow, back, succ = pl.pallas_call(
         functools.partial(kernel, (S, n, t, D)),
         out_shape=(
@@ -399,10 +445,10 @@
             jax.ShapeDtypeStruct((t, D), BF16),
             jax.ShapeDtypeStruct((r, D), BF16),
         ),
-        in_specs=[vmem] * 3,
-        out_specs=(vmem,) * 3,
+        in_specs=[held] * 3,
+        out_specs=(held,) * 3,
         scratch_shapes=[
-            pltpu.VMEM((R, D), BF16),
+            pltpu.VMEM((R, h), BF16),
             pltpu.VMEM((R, D), BF16),
             pltpu.VMEM((T, R), BF16),
             pltpu.VMEM((T, r), BF16),
@@ -423,6 +469,8 @@
             pltpu.VMEM((n, t, r), BF16),
             pltpu.VMEM((t, D), BF16),
             pltpu.VMEM((tt, h), BF16),
+            pltpu.VMEM((r, D), BF16),
+            pltpu.VMEM((t, D), BF16),
             pltpu.VMEM((n, 8, 128), F32),
             pltpu.VMEM((S, 8, 128), F32),
             pltpu.VMEM((2, 8, 128), F32),
@@ -435,6 +483,15 @@
         ),
         name="relay",
     )(acts[0], weights[0], cotangent[0])
+    blocks = [pl.BlockSpec((rows // 4, D), lambda i: (i, 0)) for rows in (t, t, r)]
+    shadow, back, succ = pl.pallas_call(
+        hand_over,
+        grid=(4,),
+        out_shape=tuple(jax.ShapeDtypeStruct(x.shape, x.dtype) for x in (shadow, back, succ)),
+        in_specs=blocks,
+        out_specs=tuple(blocks),
+        name="hand_over",
+    )(shadow, back, succ)
     return shadow[None], back[None], succ[None]
 
 

time: 125 us -> 100 us (0.80)
  Pallas kernels: 119 us -> 99.5 us
  local copies, waits for them, and re-layouts: 5.23 us -> 0 us
    pallas_call x1, Pallas kernels: 119 us -> 95.3 us  [per_device(): pl.pallas_call(functools.partial(kernel, (S, n, t, D)), out_shape=(jax.Sh...]
    unnamed x5 -> x0, local copies, waits for them, and re-layouts: 5.23 us -> none
    pallas_call x0 -> x1, Pallas kernels: none -> 4.23 us  [per_device(): pl.pallas_call(hand_over, grid=(4,), out_shape=tuple((jax.ShapeDtypeStruc...]
where the time goes in v2:
time: 100 us
  Pallas kernels  99.5 us (100%)
    pallas_call x1, Pallas kernels, per_device(): pl.pallas_call(functools.partial(kernel, (S, n, t, D)), out_shape=(jax.Sh...  95.3 us
    pallas_call x1, Pallas kernels, per_device(): pl.pallas_call(hand_over, grid=(4,), out_shape=tuple((jax.ShapeDtypeStruc...  4.23 us

profile of v2, /device:TPU:0, one launch (start us, length us, event | category | flops | bytes accessed | tf_op | source)
XLA Modules:
  0.0 100.1 jit_solution(9483606848333989146)
XLA Ops:
  0.6 95.3 %relay.1 = (bf16[128,2048]{1,0:T(8,128)(2,1)}, bf16[128,2048]{1,0:T(8,128)(2,1)}, bf16[512,2048]{1,0:T(8,128)(2,1)}) custom-call(bf16[128,2048]{1,0:T(8,128)(2,1)} %bitcast.7, bf16[512,2048]{1,0:T(8,128)(2,1)} %bitcast.6, bf16[128,2048]{1,0:T(8,128)(2,1)} %bitcast.8), custom_call_target="tpu_custom_call" | custom-call | tf_op jit(solution)/shard_map/relay/pallas_call | solution.py:441
  95.9 4.2 %hand_over.1 = (bf16[128,2048]{1,0:T(8,128)(2,1)}, bf16[128,2048]{1,0:T(8,128)(2,1)}, bf16[512,2048]{1,0:T(8,128)(2,1)}) custom-call(bf16[128,2048]{1,0:T(8,128)(2,1)} %get-tuple-element.9.a, bf16[128,2048]{1,0:T(8,128)(2,1)} %get-tuple-element.10.b, bf16[512,2048]{1,0:T(8,128)(2,1)} %get-tuple-element.11.d), custom_call_target="tpu_custom_call" | custom-call | tf_op jit(solution)/shard_map/hand_over/pallas_call | solution.py:487

commit v3 on v2

--- a/solution.py
+++ b/solution.py
@@ -108,7 +108,7 @@
     ahr, chr_ = fresh("r"), fresh("r")
     send(lambda: acts.at[:, cols(other * h, h)], lambda: ah.at[rows(c * t, t), :], ahr, partner)
     send(lambda: cot.at[:, cols(other * h, h)], lambda: ch.at[rows(c * t, t), :], chr_, partner)
-    xnr, pgr, cnr = (fresh("r") for _ in range(3))
+    xnr, cnr = fresh("r"), fresh("r")
     wnr, wnf = fresh("r", 2 * pieces), fresh("r", pieces)
     own_rows = rows(c * r, r)
 
@@ -138,29 +138,30 @@
 
     step = min(256, h)
 
-    def product(gathered, matrix, at, out, d, k, width):
+    def product(gathered, matrix, at, out, d, k, width, lo=0, size=tt):
         value = jnp.dot(
-            gathered[rows(mate(d) * tt, tt), :], matrix[:, cols(at + k * width, width)],
+            gathered[rows(mate(d) * tt + lo, size), :], matrix[:, cols(at + k * width, width)],
             preferred_element_type=F32,
         )
         if d:
-            out[d, :, cols(k * width, width)] = value.astype(BF16)
+            out[d, lo:lo + size, cols(k * width, width)] = value.astype(BF16)
         else:
-            acc[:, cols(k * width, width)] = value
-
-    f1 = fresh("r", pairs)
+            acc[lo:lo + size, cols(k * width, width)] = value
+
+    f1 = fresh("r", 2 * pairs)
     for d in list(range(1, pairs)) + [0]:
-        def body(k, carry, d=d):
-            product(xg, wp, 0, p1s, d, k, step)
-            return carry
-
-        lax.fori_loop(0, h // step, body, None)
-        if d:
-            send(lambda d=d: p1s.at[d], lambda d=d: p1r.at[d], f1 + d, (s, 2 * mate(d) + c))
+        for u in range(2):
+            def body(k, carry, d=d, u=u):
+                product(xg, wp, 0, p1s, d, k, step, u * t, t)
+                return carry
+
+            lax.fori_loop(0, h // step, body, None)
+            if d:
+                part = slice(u * t, (u + 1) * t)
+                send(lambda d=d, part=part: p1s.at[d, part], lambda d=d, part=part: p1r.at[d, part],
+                     f1 + 2 * d + u, (s, 2 * mate(d) + c))
     recv(ah.at[rows(other * t, t), :], ahr)
     recv(ch.at[rows(other * t, t), :], chr_)
-    for d in range(1, pairs):
-        recv(p1r.at[d], f1 + d)
 
     def total(landing, here):
         pre = acc[here, :]
@@ -181,30 +182,42 @@
         pgo[c, rows(q * tt + i * 16, 16), :] = (ch[here, :].astype(F32) * slope).astype(BF16)
         return carry
 
-    lax.fori_loop(0, tt // 16, act_body, None)
-
-    def block(buf, half, qq):
-        return buf.at[half, rows(qq * tt, tt), :]
-
-    send(lambda: block(pgo, c, q), lambda: block(pgn, c, q), pgr, prev, has_prev)
-    relayed = pending.pop()
-    od, of, nd, nf = (fresh("r", pairs) for _ in range(4))
-
-    def gather_start(buf, direct, forward, pred):
+    def block(buf, half, qq, u):
+        return buf.at[half, rows(qq * tt + u * t, t), :]
+
+    relayed = []
+    pgr = fresh("r", 2)
+    for u in range(2):
         for d in range(1, pairs):
-            send(lambda: block(buf, c, q), lambda: block(buf, c, q), direct + d,
-                 (s, 2 * mate(d) + c), pred)
-        send(lambda: block(buf, c, q), lambda: block(buf, c, q), forward, partner, pred)
+            recv(p1r.at[d, u * t:(u + 1) * t], f1 + 2 * d + u)
+        lax.fori_loop(u * (t // 16), (u + 1) * (t // 16), act_body, None)
+        send(lambda u=u: block(pgo, c, q, u), lambda u=u: block(pgn, c, q, u), pgr + u, prev,
+             has_prev)
+        relayed.append(pending.pop())
+
+    relay_weights(late)
+
+    od, of, nd, nf = (fresh("r", 2 * pairs) for _ in range(4))
+
+    def gather_start(buf, direct, forward, pred, u):
+        here = lambda: block(buf, c, q, u)
+        for d in range(1, pairs):
+            send(here, here, direct + 2 * d + u, (s, 2 * mate(d) + c), pred)
+        send(here, here, forward + u, partner, pred)
 
     def gather_end(buf, direct, forward, pred):
-        for d in range(1, pairs):
-            when(pred, lambda d=d: recv(block(buf, c, source(d)), direct + d))
-            send(lambda d=d: block(buf, c, source(d)), lambda d=d: block(buf, c, source(d)),
-                 forward + d, partner, pred)
-        for d in range(pairs):
-            when(pred, lambda d=d: recv(block(buf, other, source(d)), forward + d))
-
-    gather_start(pgo, od, of, first)
+        for u in range(2):
+            for d in range(1, pairs):
+                here = lambda d=d, u=u: block(buf, c, source(d), u)
+                when(pred, lambda d=d, u=u, here=here: recv(here(), direct + 2 * d + u))
+                send(here, here, forward + 2 * d + u, partner, pred)
+        for u in range(2):
+            for d in range(pairs):
+                when(pred, lambda d=d, u=u: recv(
+                    block(buf, other, source(d), u), forward + 2 * d + u))
+
+    gather_start(pgo, od, of, first, 0)
+    gather_start(pgo, od, of, first, 1)
 
     ogd, ogf = fresh("r", pairs), fresh("r", pairs)
     ours = q // half_pairs == c
@@ -278,16 +291,12 @@
         es[0] = es[0] + tile
 
     es[0] = jnp.zeros((8, 128), F32)
-    shadow_pieces(early)
-
-    @pl.when(has_next)
-    def _():
-        recv(block(pgn, c, q), pgr)
-
-    gather_start(pgn, nd, nf, has_next)
-    when(*relayed)
-    relay_weights(late)
+    for u in range(2):
+        when(has_next, lambda u=u: recv(block(pgn, c, q, u), pgr + u))
+        gather_start(pgn, nd, nf, has_next, u)
+        when(*relayed[u])
     send(lambda: cot, lambda: cn, cnr, prev, has_prev)
+
     gather_end(pgo, od, of, first)
 
     @pl.when(first)
@@ -318,6 +327,7 @@
     for d in range(1, S):
         send(lambda: es.at[1], lambda d=d: e2.at[d], e2r + d, (lax.rem(s + d, S), j))
 
+    shadow_pieces(early)
     shadow_pieces(late)
     spr_base = fresh("r", n)
 
@@ -436,7 +446,7 @@
     t, D = acts.shape[1:]
     r, pairs, h = D // n, n // 2, D // 2
     R, tt, T = 2 * r, 2 * t, n * t
-    sems = 15 * pairs + 4 * n + 2 * S + 40
+    sems = 26 * pairs + 4 * n + 2 * S + 40
     held = pl.BlockSpec(memory_space=pl.ANY)
     shadow, back, succ = pl.pallas_call(
         functools.partial(kernel, (S, n, t, D)),

time: 100 us -> 98.6 us (0.986)
  Pallas kernels: 99.5 us -> 97.8 us
    pallas_call x1, Pallas kernels: 95.3 us -> 93.5 us  [per_device(): pl.pallas_call(functools.partial(kernel, (S, n, t, D)), out_shape=(jax.Sh...]
where the time goes in v3:
time: 98.6 us; the launch traced here: 98.4 us
  Pallas kernels  97.8 us (99%)
    pallas_call x1, Pallas kernels, per_device(): pl.pallas_call(functools.partial(kernel, (S, n, t, D)), out_shape=(jax.Sh...  93.5 us
    pallas_call x1, Pallas kernels, per_device(): pl.pallas_call(hand_over, grid=(4,), out_shape=tuple((jax.ShapeDtypeStruc...  4.23 us

profile of v3, /device:TPU:0, one launch (start us, length us, event | category | flops | bytes accessed | tf_op | source)
XLA Modules:
  0.0 98.4 jit_solution(636669729947244030)
XLA Ops:
  0.6 93.5 %relay.1 = (bf16[128,2048]{1,0:T(8,128)(2,1)}, bf16[128,2048]{1,0:T(8,128)(2,1)}, bf16[512,2048]{1,0:T(8,128)(2,1)}) custom-call(bf16[128,2048]{1,0:T(8,128)(2,1)} %bitcast.7, bf16[512,2048]{1,0:T(8,128)(2,1)} %bitcast.6, bf16[128,2048]{1,0:T(8,128)(2,1)} %bitcast.8), custom_call_target="tpu_custom_call" | custom-call | tf_op jit(solution)/shard_map/relay/pallas_call | solution.py:451
  94.2 4.2 %hand_over.1 = (bf16[128,2048]{1,0:T(8,128)(2,1)}, bf16[128,2048]{1,0:T(8,128)(2,1)}, bf16[512,2048]{1,0:T(8,128)(2,1)}) custom-call(bf16[128,2048]{1,0:T(8,128)(2,1)} %get-tuple-element.9.a, bf16[128,2048]{1,0:T(8,128)(2,1)} %get-tuple-element.10.b, bf16[512,2048]{1,0:T(8,128)(2,1)} %get-tuple-element.11.d), custom_call_target="tpu_custom_call" | custom-call | tf_op jit(solution)/shard_map/hand_over/pallas_call | solution.py:497
